TPU v7x, 32 devices: a whole 2x2x4 slice. The times are simulated.
32 devices in a mesh: groups: 2 (over x), wide: 16 (over z, y, core).
Axes of the slice: x: 2, y: 2, z: 4, core: 2. Of those that a mesh axis runs over, the one named last changes fastest.
Arguments:
- features: float32 [4, 32, 16, 256], P('groups', 'wide'), parts along dimension 0, may hold values from -6 to 6
- first_weight: float32 [3, 3, 256, 256], replicated, may hold values from -0.125 to 0.125
- down_weight: float32 [2, 2, 256, 1024], replicated, may hold values from -0.1875 to 0.1875
- inner_weight: float32 [1, 3, 3, 1024, 1024], P(None, None, None, None, 'wide'), may hold values from -0.0625 to 0.0625
- outer_weight: float32 [1, 3, 3, 1024, 1024], P(None, None, None, None, 'wide'), may hold values from -0.0625 to 0.0625
Outputs:
- refined: float32 [4, 16, 8, 1024], P('groups', None, None, 'wide'), parts along dimension 0
There are 2 independent parts, one for each index of `groups`. A program takes and returns all parts, laid end to end along the dimension named above; an argument that names none is the same for every part. Nothing has to cross between parts.
All inputs are finite; a program needn't handle non-finite values.
Results may differ from a plain program's by a relative error of at most 0.00013.
Values sent between devices are 32-bit elements; how exact they have to be, the bound alone decides.
A program may use at most 64 MiB of HBM per device.

v0:
```python
import jax
import jax.numpy as jnp
from jax import lax
from jax.sharding import PartitionSpec as P


def extended_2(shard, sides, width):
    for axis, dim in sides:
        size, length = (lax.axis_size(axis), shard.shape[dim])
        up = [(i, (i + 1) % size) for i in range(size - 1)]
        down = [(j, i) for i, j in up]
        last = lax.slice_in_dim(shard, length - width, length, axis=dim)
        first = lax.slice_in_dim(shard, 0, width, axis=dim)
        before = lax.ppermute(last, axis, up)
        after = lax.ppermute(first, axis, down)
        shard = jnp.concatenate([before, shard, after], axis=dim)
    return shard


def partner_2(block, axis, distance):
    count = lax.axis_size(axis)
    route = []
    for low in range(count):
        high = low | 1 << distance
        if high != low and high < count:
            route += [(low, high), (high, low)]
    return lax.ppermute(block, axis, route)


def convolve(feature_map, kernel, layout, strides, padding):
    return lax.conv_general_dilated(
        feature_map,
        kernel,
        strides,
        padding,
        dimension_numbers=("NHWC", layout, "NHWC"),
        precision=lax.Precision.HIGHEST,
    )


def device_bit(bit_number):
    return lax.axis_index("wide") >> bit_number & 1


def spatial(local_rows, first_weight, down_weight):
    extended = extended_2(local_rows, (("wide", 1),), 1)
    activated = jax.nn.relu(convolve(extended, first_weight, "HWIO", (1, 1), [(0, 0), (1, 1)]))
    return convolve(activated, down_weight, "HWIO", (2, 2), "VALID")


def weight_blocks(stacked, grid_size, low_bits):
    leading = stacked.shape[:-2]
    width = stacked.shape[-2]
    narrow = stacked.shape[-1]
    slots = jnp.moveaxis(stacked.reshape(leading + (grid_size, width // grid_size, narrow)), -3, 0)
    remainder = slots.shape[1:]
    for bit_number in low_bits:
        paired = slots.reshape((grid_size >> bit_number + 1, 2, 1 << bit_number) + remainder)
        lower = paired[:, 0]
        upper = paired[:, 1]
        first_half = device_bit(bit_number) == 0
        outgoing = jnp.where(first_half, upper, lower)
        keeping = jnp.where(first_half, lower, upper)
        incoming = partner_2(outgoing, "wide", bit_number)
        merged = jnp.stack(
            [jnp.where(first_half, keeping, incoming), jnp.where(first_half, incoming, keeping)], 1
        )
        slots = merged.reshape((grid_size,) + remainder)
    joined = jnp.moveaxis(slots, 0, -2)
    return joined.reshape(leading + (width // grid_size, grid_size * narrow))


def channel_pieces(piece, low_bits):
    for bit_number in low_bits:
        partner = partner_2(piece, "wide", bit_number)
        first_half = device_bit(bit_number) == 0
        piece = jnp.where(
            first_half, jnp.concatenate([piece, partner], 3), jnp.concatenate([partner, piece], 3)
        )
    return piece


def group_total(partial_value, bit_list):
    for bit_number in bit_list:
        partial_value = partial_value + partner_2(partial_value, "wide", bit_number)
    return partial_value


def body(features, first_weight, down_weight, inner_weight, outer_weight):
    total_bits = lax.axis_size("wide").bit_length() - 1
    half_bits = total_bits // 2
    grid_size = 1 << half_bits
    low_bits = list(range(half_bits))
    high_bits = list(range(half_bits, total_bits))
    channels = down_weight.shape[3]
    stacked = weight_blocks(jnp.stack([inner_weight, outer_weight], 0), grid_size, low_bits)
    reduced = spatial(features, first_weight, down_weight)
    current = channel_pieces(
        lax.all_to_all(reduced, "wide", split_axis=3, concat_axis=1, tiled=True), low_bits
    )
    kernel_in = stacked[0, 0]
    kernel_out = stacked[1, 0]
    partial_value = convolve(current, kernel_in, "HWOI", (1, 1), "SAME")
    hidden = jax.nn.relu(group_total(partial_value, high_bits))
    partial_value = convolve(hidden, kernel_out, "HWIO", (1, 1), "SAME")
    current = jax.nn.relu(current + group_total(partial_value, low_bits))
    own_count = channels // lax.axis_size("wide")
    offset = lax.axis_index("wide") % grid_size * own_count
    return lax.dynamic_slice_in_dim(current, offset, own_count, 3)


def solution(mesh):
    in_specs = (
        P("groups", "wide", None, None),
        P(),
        P(),
        P(None, None, None, None, "wide"),
        P(None, None, None, None, "wide"),
    )
    out_specs = P("groups", None, None, "wide")
    return jax.shard_map(body, mesh=mesh, in_specs=in_specs, out_specs=out_specs, check_vma=False)
```

profile of v0, /device:TPU:1, one launch (start us, length us, event | category | flops | bytes accessed | tf_op | source)
XLA Modules:
  0.0 160.1 jit_solution(14585305848927858681)
XLA Ops:
  0.0 3.8 %stack.27 = f32[1,1,3,3,4,256,64]{5,4,6,3,2,1,0:T(4,128)} reshape(f32[1,3,3,1024,64]{3,4,2,1,0:T(8,128)} %param.8) | data formatting | bytes 4718592 | tf_op jit(solution)/shard_map/stack | solution.py:96
  3.8 3.7 %stack.28 = f32[1,1,3,3,4,256,64]{5,4,6,3,2,1,0:T(4,128)} reshape(f32[1,3,3,1024,64]{3,4,2,1,0:T(8,128)} %param.9) | data formatting | bytes 4718592 | tf_op jit(solution)/shard_map/stack | solution.py:96
  7.5 3.5 %maximum_bitcast_fusion = f32[4,2,1,3,3,256,64]{5,0,6,4,3,2,1:T(4,128)S(1)} fusion(f32[1,1,3,3,4,256,64]{5,4,6,3,2,1,0:T(4,128)} %stack.28, f32[1,1,3,3,4,256,64]{5,4,6,3,2,1,0:T(4,128)} %stack.27), kind=kLoop, calls=%fused_computation | loop fusion | flops 1179648 | bytes 9437184 | tf_op jit(solution)/shard_map/transpose | solution.py:55
  11.9 2.2 %select_bitcast_fusion.5 = f32[2,1,2,1,3,3,256,64]{6,7,5,4,2,0,3,1:T(8,128)} fusion(f32[2,2,1,2,1,3,3,256,64]{7,8,6,5,4,3,2,1,0:T(8,128)S(1)} %bitcast.103, pred[]{:T(512)S(6)} %eq.11), kind=kLoop, calls=%fused_computation.13 | loop fusion | flops 589824 | bytes 7077889 | tf_op jit(solution)/shard_map/jit(_where)/select_n | solution.py:62
  14.9 4.8 %collective-permute-done.4 = f32[2,1,2,1,3,3,256,64]{6,7,5,4,2,0,3,1:T(8,128)} collective-permute-done((f32[2,1,2,1,3,3,256,64]{6,7,5,4,2,0,3,1:T(8,128)}, f32[2,1,2,1,3,3,256,64]{6,7,5,4,2,0,3,1:T(8,128)}, u32[]{:S(2)}, u32[]{:S(2)}) %collective-permute-start.4) | collective-permute-done | bytes 2359328 | tf_op jit(solution)/shard_map/ppermute | solution.py:27
  19.7 3.9 %select_bitcast_fusion.4 = (f32[2,1,1,2,1,3,3,256,64]{7,8,6,5,3,0,4,2,1:T(8,128)S(1)}, f32[2,1,1,2,1,3,3,256,64]{7,8,6,5,3,0,4,2,1:T(8,128)S(1)}) fusion(f32[2,1,2,1,3,3,256,64]{6,7,5,4,2,0,3,1:T(8,128)} %collective-permute-done.4, pred[]{:T(512)S(6)} %eq.11, f32[2,2,1,2,1,3,3,256,64]{7,8,6,5,4,3,2,1,0:T(8,128)} %bitcast.104), kind=kLoop, calls=%fused_computation.12 | loop fusion | flops 1769472 | bytes 11797504 | tf_op jit(solution)/shard_map/stack | solution.py:65
  24.2 2.2 %select_bitcast_fusion.2 = f32[1,2,2,1,3,3,256,64]{6,7,5,4,2,1,3,0:T(8,128)} fusion(f32[1,2,2,2,1,3,3,256,64]{7,8,6,5,3,1,2,4,0:T(8,128)S(1)} %maximum_bitcast_fusion.1, pred[]{:T(512)S(6)} %eq.10), kind=kLoop, calls=%fused_computation.10 | loop fusion | flops 589824 | bytes 7077889 | tf_op jit(solution)/shard_map/jit(_where)/select_n | solution.py:62
  27.1 2.4 %collective-permute-start.5 = (f32[1,2,2,1,3,3,256,64]{6,7,5,4,2,1,3,0:T(8,128)}, f32[1,2,2,1,3,3,256,64]{6,7,5,4,2,1,3,0:T(8,128)}, u32[]{:S(2)}, u32[]{:S(2)}) collective-permute-start(f32[1,2,2,1,3,3,256,64]{6,7,5,4,2,1,3,0:T(8,128)} %select_bitcast_fusion.2), channel_id=1, source_target_pairs={{0,2},{2,0},{1,3},{3,1},{4,6},{6,4},{5,7},{7,5},{8,10},{10,8},{9,1... | collective-permute-start | bytes 7077896 | tf_op jit(solution)/shard_map/ppermute | solution.py:27
  29.5 2.2 %collective-permute-start = (f32[2,1,16,256]{3,2,1,0:T(8,128)S(1)}, f32[2,1,16,256]{3,2,1,0:T(8,128)S(1)}, u32[]{:S(2)}, u32[]{:S(2)}) collective-permute-start(f32[2,1,16,256]{3,2,1,0:T(8,128)S(1)} %get-tuple-element.11), channel_id=1, source_target_pairs={{0,1},{1,2},{2,3},{3,4},{4,5},{5,6},{6,7},{7,8},{8,9},{9,10},{10,1... | collective-permute-start | bytes 98312 | tf_op jit(solution)/shard_map/ppermute | solution.py:14
  31.7 2.2 %collective-permute-start.1 = (f32[2,1,16,256]{3,2,1,0:T(8,128)S(1)}, f32[2,1,16,256]{3,2,1,0:T(8,128)S(1)}, u32[]{:S(2)}, u32[]{:S(2)}) collective-permute-start(f32[2,1,16,256]{3,2,1,0:T(8,128)S(1)} %get-tuple-element.12), channel_id=1, source_target_pairs={{1,0},{2,1},{3,2},{4,3},{5,4},{6,5},{7,6},{8,7},{9,8},{10,9},{11,1... | collective-permute-start | bytes 98312 | tf_op jit(solution)/shard_map/ppermute | solution.py:15
  33.8 47.2 %collective-permute-done = f32[2,1,16,256]{3,2,1,0:T(8,128)S(1)} collective-permute-done((f32[2,1,16,256]{3,2,1,0:T(8,128)S(1)}, f32[2,1,16,256]{3,2,1,0:T(8,128)S(1)}, u32[]{:S(2)}, u32[]{:S(2)}) %collective-permute-start) | collective-permute-done | bytes 32800 | tf_op jit(solution)/shard_map/ppermute | solution.py:14
  82.0 1.3 fusion.3
  83.9 2.1 %convolution_bitcast_fusion = f32[2,1,8,1024]{3,2,0,1:T(8,128)S(1)} fusion(f32[2,2,256,1024]{3,2,1,0:T(8,128)S(1)} %copy-done.4, f32[2,2,8,3,256]{4,1,3,2,0:T(2,128)S(1)} %fusion.12), kind=kOutput, calls=%fused_computation.17 | convolution fusion | flops 201326592 | bytes 4358144 | tf_op jit(solution)/shard_map/conv_general_dilated | solution.py:31
  86.5 1.6 reshape.128
  88.1 12.1 %all_to_all.18 = f32[16,1,1024]{2,1,0:T(1,128)S(1)} all-to-all(f32[16,1,1024]{2,1,0:T(1,128)S(1)} %reshape.128), channel_id=1, replica_groups=mesh['groups'=2,'wide'=16] {'wide'}, dimensions={0} | all-to-all | bytes 131072 | tf_op jit(solution)/shard_map/all_to_all | solution.py:99
  101.6 1.6 reshape.129
  106.2 4.7 %collective-permute-done.3 = f32[2,16,8,128]{3,0,2,1:T(2,128)S(1)} collective-permute-done((f32[2,16,8,128]{3,0,2,1:T(2,128)S(1)}, f32[2,16,8,128]{3,0,2,1:T(2,128)S(1)}, u32[]{:S(2)}, u32[]{:S(2)}) %collective-permute-start.3) | collective-permute-done | bytes 131104 | tf_op jit(solution)/shard_map/ppermute | solution.py:27
  111.1 4.2 %select_bitcast_fusion.1 = (f32[1,1,2,2,1,3,3,256,64]{7,8,6,5,3,2,4,1,0:T(8,128)S(1)}, f32[1,1,2,2,1,3,3,256,64]{7,8,6,5,3,2,4,1,0:T(8,128)S(1)}) fusion(f32[1,2,2,1,3,3,256,64]{6,7,5,4,2,1,3,0:T(8,128)} %collective-permute-done.5, pred[]{:T(512)S(6)} %eq.10, f32[1,2,2,2,1,3,3,256,64]{7,8,6,5,3,1,2,4,0:T(8,128)} %copy-done.2), kind=kLoop, calls=%fused_computation.9 | loop fusion | flops 1769472 | bytes 11797504 | tf_op jit(solution)/shard_map/stack | solution.py:65
  117.1 5.3 %fusion.18 = f32[2,16,8,256]{3,0,2,1:T(2,128)S(1)} fusion(f32[2,16,8,256]{3,0,2,1:T(2,128)S(1)} %maximum_select_fusion, f32[3,3,256,256]{2,3,1,0:T(8,128)S(1)} %bitcast.107), kind=kOutput, calls=%fused_computation.39 | convolution fusion | flops 1591738368 | bytes 2883584 | tf_op jit(solution)/shard_map/conv_general_dilated | solution.py:31
  122.4 6.6 %collective-permute-done.6 = f32[2,16,8,256]{3,0,2,1:T(2,128)S(1)} collective-permute-done((f32[2,16,8,256]{3,0,2,1:T(2,128)S(1)}, f32[2,16,8,256]{3,0,2,1:T(2,128)S(1)}, u32[]{:S(2)}, u32[]{:S(2)}) %collective-permute-start.6) | collective-permute-done | bytes 262176 | tf_op jit(solution)/shard_map/ppermute | solution.py:27
  129.3 14.6 %collective-permute-done.7 = f32[2,16,8,256]{3,0,2,1:T(2,128)S(1)} collective-permute-done((f32[2,16,8,256]{3,0,2,1:T(2,128)S(1)}, f32[2,16,8,256]{3,0,2,1:T(2,128)S(1)}, u32[]{:S(2)}, u32[]{:S(2)}) %collective-permute-start.7) | collective-permute-done | bytes 262176 | tf_op jit(solution)/shard_map/ppermute | solution.py:27
  143.9 5.7 %fusion.7 = f32[2,16,8,256]{3,0,2,1:T(2,128)S(1)} fusion(f32[3,3,256,256]{2,3,1,0:T(8,128)S(1)} %bitcast.110, f32[2,16,8,256]{3,0,2,1:T(2,128)S(1)} %add.22, f32[2,16,8,256]{3,0,2,1:T(2,128)S(1)} %collective-permute-done.7), kind=kOutput, calls=%fused_computation.23 | convolution fusion | flops 1591869440 | bytes 3145728 | tf_op jit(solution)/shard_map/conv_general_dilated | solution.py:31
  150.1 1.2 collective-permute-done.8
  151.5 7.5 %collective-permute-done.9 = f32[2,16,8,256]{3,0,2,1:T(2,128)S(1)} collective-permute-done((f32[2,16,8,256]{3,0,2,1:T(2,128)S(1)}, f32[2,16,8,256]{3,0,2,1:T(2,128)S(1)}, u32[]{:S(2)}, u32[]{:S(2)}) %collective-permute-start.9) | collective-permute-done | bytes 262176 | tf_op jit(solution)/shard_map/ppermute | solution.py:27
  (50 shorter events, 13.6 us)
Async XLA Ops:
  0.0 82.0 %copy-start = (f32[3,3,256,256]{3,2,1,0:T(8,128)S(1)}, f32[3,3,256,256]{3,2,1,0:T(8,128)}, u32[]{:S(2)}) copy-start(f32[3,3,256,256]{3,2,1,0:T(8,128)} %param.6) | copy-start | bytes 7077892
  11.9 2.9 %copy-start.3 = (f32[4,2,1,3,3,256,64]{5,6,4,3,2,1,0:T(8,128)}, f32[4,2,1,3,3,256,64]{5,6,4,3,2,1,0:T(8,128)S(1)}, u32[]{:S(2)}) copy-start(f32[4,2,1,3,3,256,64]{5,6,4,3,2,1,0:T(8,128)S(1)} %copy.63) | copy-start | bytes 14155780
  14.8 4.9 %collective-permute-start.4 = (f32[2,1,2,1,3,3,256,64]{6,7,5,4,2,0,3,1:T(8,128)}, f32[2,1,2,1,3,3,256,64]{6,7,5,4,2,0,3,1:T(8,128)}, u32[]{:S(2)}, u32[]{:S(2)}) collective-permute-start(f32[2,1,2,1,3,3,256,64]{6,7,5,4,2,0,3,1:T(8,128)} %select_bitcast_fusion.5), channel_id=1, source_target_pairs={{0,1},{1,0},{2,3},{3,2},{4,5},{5,4},{6,7},{7,6},{8,9},{9,8},{10,11... | collective-permute-start | bytes 7077896 | tf_op jit(solution)/shard_map/ppermute | solution.py:27
  24.2 3.0 %copy-start.2 = (f32[1,2,2,2,1,3,3,256,64]{7,8,6,5,3,1,2,4,0:T(8,128)}, f32[1,2,2,2,1,3,3,256,64]{7,8,6,5,3,1,2,4,0:T(8,128)S(1)}, u32[]{:S(2)}) copy-start(f32[1,2,2,2,1,3,3,256,64]{7,8,6,5,3,1,2,4,0:T(8,128)S(1)} %maximum_bitcast_fusion.1) | copy-start | bytes 14155780
  24.2 5.3 %copy-start.5 = (f32[2,2,16,256]{3,2,1,0:T(8,128)S(1)}, f32[2,2,16,256]{3,2,1,0:T(8,128)}, u32[]{:S(2)}) copy-start(f32[2,2,16,256]{3,2,1,0:T(8,128)} %param.5) | copy-start | bytes 196612
  24.2 57.8 %copy-start.6 = (pred[16,3]{0,1:T(4,128)(4,1)S(1)}, pred[16,3]{0,1:T(4,128)(4,1)}, u32[]{:S(2)}) copy-start(pred[16,3]{0,1:T(4,128)(4,1)} %constant.38) | copy-start | bytes 148
  27.1 84.0 %collective-permute-start.5 = (f32[1,2,2,1,3,3,256,64]{6,7,5,4,2,1,3,0:T(8,128)}, f32[1,2,2,1,3,3,256,64]{6,7,5,4,2,1,3,0:T(8,128)}, u32[]{:S(2)}, u32[]{:S(2)}) collective-permute-start(f32[1,2,2,1,3,3,256,64]{6,7,5,4,2,1,3,0:T(8,128)} %select_bitcast_fusion.2), channel_id=1, source_target_pairs={{0,2},{2,0},{1,3},{3,1},{4,6},{6,4},{5,7},{7,5},{8,10},{10,8},{9,1... | collective-permute-start | bytes 7077896 | tf_op jit(solution)/shard_map/ppermute | solution.py:27
  29.5 51.5 %collective-permute-start = (f32[2,1,16,256]{3,2,1,0:T(8,128)S(1)}, f32[2,1,16,256]{3,2,1,0:T(8,128)S(1)}, u32[]{:S(2)}, u32[]{:S(2)}) collective-permute-start(f32[2,1,16,256]{3,2,1,0:T(8,128)S(1)} %get-tuple-element.11), channel_id=1, source_target_pairs={{0,1},{1,2},{2,3},{3,4},{4,5},{5,6},{6,7},{7,8},{8,9},{9,10},{10,1... | collective-permute-start | bytes 98312 | tf_op jit(solution)/shard_map/ppermute | solution.py:14
  31.7 49.9 %collective-permute-start.1 = (f32[2,1,16,256]{3,2,1,0:T(8,128)S(1)}, f32[2,1,16,256]{3,2,1,0:T(8,128)S(1)}, u32[]{:S(2)}, u32[]{:S(2)}) collective-permute-start(f32[2,1,16,256]{3,2,1,0:T(8,128)S(1)} %get-tuple-element.12), channel_id=1, source_target_pairs={{1,0},{2,1},{3,2},{4,3},{5,4},{6,5},{7,6},{8,7},{9,8},{10,9},{11,1... | collective-permute-start | bytes 98312 | tf_op jit(solution)/shard_map/ppermute | solution.py:15
  81.7 2.2 %copy-start.4 = (f32[2,2,256,1024]{3,2,1,0:T(8,128)S(1)}, f32[2,2,256,1024]{3,2,1,0:T(8,128)}, u32[]{:S(2)}) copy-start(f32[2,2,256,1024]{3,2,1,0:T(8,128)} %param.7) | copy-start | bytes 12582916
  103.8 2.0 %collective-permute-start.2 = (f32[2,16,8,64]{3,0,2,1:T(2,128)S(1)}, f32[2,16,8,64]{3,0,2,1:T(2,128)S(1)}, u32[]{:S(2)}, u32[]{:S(2)}) collective-permute-start(f32[2,16,8,64]{3,0,2,1:T(2,128)S(1)} %bitcast.113), channel_id=1, source_target_pairs={{0,1},{1,0},{2,3},{3,2},{4,5},{5,4},{6,7},{7,6},{8,9},{9,8},{10,11... | collective-permute-start | bytes 196616 | tf_op jit(solution)/shard_map/ppermute | solution.py:27
  106.1 4.8 %collective-permute-start.3 = (f32[2,16,8,128]{3,0,2,1:T(2,128)S(1)}, f32[2,16,8,128]{3,0,2,1:T(2,128)S(1)}, u32[]{:S(2)}, u32[]{:S(2)}) collective-permute-start(f32[2,16,8,128]{3,0,2,1:T(2,128)S(1)} %maximum_select_fusion.1), channel_id=1, source_target_pairs={{0,2},{2,0},{1,3},{3,1},{4,6},{6,4},{5,7},{7,5},{8,10},{10,8},{9,1... | collective-permute-start | bytes 393224 | tf_op jit(solution)/shard_map/ppermute | solution.py:27
  122.4 6.7 %collective-permute-start.6 = (f32[2,16,8,256]{3,0,2,1:T(2,128)S(1)}, f32[2,16,8,256]{3,0,2,1:T(2,128)S(1)}, u32[]{:S(2)}, u32[]{:S(2)}) collective-permute-start(f32[2,16,8,256]{3,0,2,1:T(2,128)S(1)} %fusion.18), channel_id=1, source_target_pairs={{0,4},{4,0},{1,5},{5,1},{2,6},{6,2},{3,7},{7,3},{8,12},{12,8},{9,1... | collective-permute-start | bytes 786440 | tf_op jit(solution)/shard_map/ppermute | solution.py:27
  129.2 14.7 %collective-permute-start.7 = (f32[2,16,8,256]{3,0,2,1:T(2,128)S(1)}, f32[2,16,8,256]{3,0,2,1:T(2,128)S(1)}, u32[]{:S(2)}, u32[]{:S(2)}) collective-permute-start(f32[2,16,8,256]{3,0,2,1:T(2,128)S(1)} %add.22), channel_id=1, source_target_pairs={{0,8},{8,0},{1,9},{9,1},{2,10},{10,2},{3,11},{11,3},{4,12},{12,4},... | collective-permute-start | bytes 786440 | tf_op jit(solution)/shard_map/ppermute | solution.py:27
  143.9 16.3 %copy-start.1 = (f32[3,3,256,256]{3,2,1,0:T(8,128)S(1)}, f32[3,3,256,256]{3,2,1,0:T(8,128)}, u32[]{:S(2)}) copy-start(f32[3,3,256,256]{3,2,1,0:T(8,128)} %param.6) | copy-start | bytes 7077892
  149.5 1.7 %collective-permute-start.8 = (f32[2,16,8,256]{3,0,2,1:T(2,128)S(1)}, f32[2,16,8,256]{3,0,2,1:T(2,128)S(1)}, u32[]{:S(2)}, u32[]{:S(2)}) collective-permute-start(f32[2,16,8,256]{3,0,2,1:T(2,128)S(1)} %fusion.7), channel_id=1, source_target_pairs={{0,1},{1,0},{2,3},{3,2},{4,5},{5,4},{6,7},{7,6},{8,9},{9,8},{10,11... | collective-permute-start | bytes 786440 | tf_op jit(solution)/shard_map/ppermute | solution.py:27
  151.4 7.6 %collective-permute-start.9 = (f32[2,16,8,256]{3,0,2,1:T(2,128)S(1)}, f32[2,16,8,256]{3,0,2,1:T(2,128)S(1)}, u32[]{:S(2)}, u32[]{:S(2)}) collective-permute-start(f32[2,16,8,256]{3,0,2,1:T(2,128)S(1)} %add.24), channel_id=1, source_target_pairs={{0,2},{2,0},{1,3},{3,1},{4,6},{6,4},{5,7},{7,5},{8,10},{10,8},{9,1... | collective-permute-start | bytes 786440 | tf_op jit(solution)/shard_map/ppermute | solution.py:27
where the time goes:
time: 162 us; the launch traced here: 160 us
  waiting for transfers between devices  88.1 us (54%)
  other arithmetic  19.3 us (12%)
  local copies, waits for them, and re-layouts  17.3 us (11%)
  matrix products  14.3 us (9%)
  blocking collectives  12.1 us (7%)
  starting transfers between devices  8.66 us (5%)
    ppermute x1, waiting for transfers between devices, extended_2(): before = lax.ppermute(last, axis, up)  47.2 us
    ppermute x8, waiting for transfers between devices, partner_2(): return lax.ppermute(block, axis, route)  40.4 us
    conv_general_dilated x4, matrix products, convolve(): lax.conv_general_dilated(feature_map, kernel, strides, padding, dimension...  14.3 us
    all_to_all x1, blocking collectives, body(): lax.all_to_all(reduced, 'wide', split_axis=3, concat_axis=1, tiled=True)  12.1 us
    another operation x3, other arithmetic, weight_blocks(): jnp.stack([jnp.where(first_half, keeping, incoming), jnp.where(first_half...  8.64 us
    another operation x2, local copies, waits for them, and re-layouts, body(): jnp.stack([inner_weight, outer_weight], 0)  7.52 us
    unnamed x17, local copies, waits for them, and re-layouts  5.22 us
    select_n x2, other arithmetic, weight_blocks(): outgoing = jnp.where(first_half, upper, lower)  4.39 us
  transfers between devices with their start and end apart: 10, of which 9 were waited for; matrix products, arithmetic and copies ran while one was open for 6% of the time, Pallas kernels for 0%

commit v1 on v0

--- a/solution.py
+++ b/solution.py
@@ -1,6 +1,10 @@
+import functools
+
 import jax
 import jax.numpy as jnp
 from jax import lax
+from jax.experimental import pallas as pl
+from jax.experimental.pallas import tpu as pltpu
 from jax.sharding import PartitionSpec as P
 
 
@@ -108,6 +112,396 @@
     offset = lax.axis_index("wide") % grid_size * own_count
     return lax.dynamic_slice_in_dim(current, offset, own_count, 3)
 
+MESH = pl.DeviceIdType.MESH
+F32 = jnp.float32
+BF16 = jnp.bfloat16
+
+
+def halves(value):
+    high = value.astype(BF16)
+    return high, (value - high.astype(F32)).astype(BF16)
+
+
+def dot(a, b):
+    return jnp.dot(a, b, preferred_element_type=F32)
+
+
+def fused(
+    wide,
+    feat_hbm, first_hbm, down_hbm, inner_hbm, outer_hbm, out_ref,
+    feat, first, down, inner, outer,
+    first_hi, first_lo, down_hi, down_lo, inner_hi, inner_lo, outer_all,
+    halo, ext, cols1, act, cols2, red, gathered, ext2, cols3,
+    part, scat, hid, taps_out, mine, theirs,
+    local_sem, halo_send, halo_recv, weight_send, weight_recv,
+    a2a_send, a2a_recv, rs_send, rs_recv, ag_send, ag_recv, fin_send, fin_recv,
+):
+    me = lax.axis_index("wide")
+    core = lax.rem(me, 2)
+    chip = lax.div(me, 2)
+    mate = me + 1 - 2 * core
+    chips = wide // 2
+    fields, rows, columns, ch = feat.shape
+    own = inner.shape[2]
+    half = inner.shape[3]
+    pair = 2 * own
+    out_cols = columns // 2
+    field_pos = wide * out_cols
+    block = inner_hi.shape[2]
+    per_block = block // own
+    blocks = half // block
+
+    def remote(src, dst, send, recv, device):
+        return pltpu.make_async_remote_copy(
+            src_ref=src, dst_ref=dst, send_sem=send, recv_sem=recv,
+            device_id={"wide": device}, device_id_type=MESH,
+        )
+
+    my_half = pl.ds(pl.multiple_of(core * half, half), half)
+    mate_half = pl.ds(pl.multiple_of((1 - core) * half, half), half)
+    local = [
+        pltpu.make_async_copy(feat_hbm, feat, local_sem.at[0]),
+        pltpu.make_async_copy(first_hbm, first, local_sem.at[1]),
+        pltpu.make_async_copy(down_hbm, down, local_sem.at[2]),
+        pltpu.make_async_copy(inner_hbm.at[:, :, my_half], inner.at[core], local_sem.at[3]),
+        pltpu.make_async_copy(outer_hbm.at[:, :, my_half], outer.at[core], local_sem.at[4]),
+    ]
+    for copy in local:
+        copy.start()
+
+    barrier = pltpu.get_barrier_semaphore()
+
+    def greet(k, carry):
+        pl.semaphore_signal(
+            barrier, inc=1, device_id={"wide": lax.rem(me + k, wide)}, device_id_type=MESH
+        )
+        return carry
+
+    lax.fori_loop(1, wide, greet, 0)
+    ext[...] = jnp.zeros_like(ext)
+    ext2[...] = jnp.zeros_like(ext2)
+    local[0].wait()
+    pl.semaphore_wait(barrier, wide - 1)
+
+    down_copy = remote(feat.at[:, rows - 1], halo.at[0], halo_send.at[0], halo_recv.at[0], me + 1)
+    up_copy = remote(feat.at[:, 0], halo.at[1], halo_send.at[1], halo_recv.at[1], me - 1)
+
+    @pl.when(me < wide - 1)
+    def _():
+        down_copy.start()
+
+    @pl.when(me > 0)
+    def _():
+        up_copy.start()
+
+    swap = [
+        remote(inner_hbm.at[:, :, mate_half], inner.at[core], weight_send.at[0], weight_recv.at[0], mate),
+        remote(outer_hbm.at[:, :, mate_half], outer.at[core], weight_send.at[1], weight_recv.at[1], mate),
+    ]
+    for copy in swap:
+        copy.start()
+
+    ext[:, 1 : rows + 1, 8 : 8 + columns, :] = feat[...]
+    local[1].wait()
+    taps = first.shape[0]
+    for t in range(taps):
+        high, low = halves(first[t])
+        first_hi[t * ch : (t + 1) * ch, :] = high
+        first_lo[t * ch : (t + 1) * ch, :] = low
+    local[2].wait()
+    for t in range(down.shape[0]):
+        high, low = halves(down[t])
+        down_hi[t * ch : (t + 1) * ch, :] = high
+        down_lo[t * ch : (t + 1) * ch, :] = low
+
+    @pl.when(me > 0)
+    def _():
+        down_copy.wait_recv()
+        ext[:, 0, 8 : 8 + columns, :] = halo[0]
+
+    @pl.when(me < wide - 1)
+    def _():
+        up_copy.wait_recv()
+        ext[:, rows + 1, 8 : 8 + columns, :] = halo[1]
+
+    count = fields * rows * columns
+    for t in range(taps):
+        dr, dc = divmod(t, 3)
+        slab = ext[:, dr : dr + rows, 7 + dc : 7 + dc + columns, :].reshape(count, ch)
+        high, low = halves(slab)
+        cols1[0:count, t * ch : (t + 1) * ch] = high
+        cols1[count : 2 * count, t * ch : (t + 1) * ch] = low
+    both = dot(cols1[...], first_hi[...])
+    activated = both[0:count] + both[count : 2 * count] + dot(cols1[0:count, :], first_lo[...])
+    activated = jnp.maximum(activated, 0.0)
+    lanes = act.shape[2]
+    for piece in range(ch // lanes):
+        act[piece] = activated[:, piece * lanes : (piece + 1) * lanes]
+    small = fields * out_cols
+    for t in range(down.shape[0]):
+        dr, dc = divmod(t, 2)
+        for piece in range(ch // lanes):
+            got = jnp.concatenate(
+                [
+                    act[piece, pl.ds((f * rows + dr) * columns + dc, out_cols, stride=2), :]
+                    for f in range(fields)
+                ],
+                axis=0,
+            )
+            high, low = halves(got)
+            at = t * ch + piece * lanes
+            cols2[0:small, at : at + lanes] = high
+            cols2[small : 2 * small, at : at + lanes] = low
+    both = dot(cols2[...], down_hi[...])
+    reduced = both[0:small] + both[small : 2 * small] + dot(cols2[0:small, :], down_lo[...])
+    for c in range(chips):
+        red[c] = reduced[:, c * pair : (c + 1) * pair]
+
+    def a2a(k):
+        to = lax.rem(me + k, wide)
+        return remote(red.at[lax.div(to, 2)], gathered.at[me], a2a_send.at[k], a2a_recv.at[me], to)
+
+    def a2a_start(k, carry):
+        a2a(k).start()
+        return carry
+
+    lax.fori_loop(1, wide, a2a_start, 0)
+    gathered[me] = red[chip]
+
+    local[3].wait()
+    swap[0].wait_recv()
+    for t in range(taps):
+        for q in range(2):
+            high, low = halves(inner[q, t])
+            at = t * pair + q * own
+            for b in range(blocks):
+                inner_hi[b, at : at + own, :] = high[:, b * block : (b + 1) * block]
+                inner_lo[b, at : at + own, :] = low[:, b * block : (b + 1) * block]
+
+    def a2a_wait(k, carry):
+        source = lax.rem(me + k, wide)
+        remote(red.at[0], gathered.at[source], a2a_send.at[k], a2a_recv.at[source], source).wait_recv()
+        return carry
+
+    lax.fori_loop(1, wide, a2a_wait, 0)
+
+    for f in range(fields):
+        ext2[f, 1 : wide + 1, 8 : 8 + out_cols, :] = gathered[:, f * out_cols : (f + 1) * out_cols, :]
+    total = fields * field_pos
+    for t in range(taps):
+        dr, dc = divmod(t, 3)
+        slab = ext2[:, dr : dr + wide, 7 + dc : 7 + dc + out_cols, :].reshape(total, pair)
+        high, low = halves(slab)
+        cols3[0:total, t * pair : (t + 1) * pair] = high
+        cols3[total : 2 * total, t * pair : (t + 1) * pair] = low
+
+    my_block = lax.div(chip, per_block)
+
+    def rs(c):
+        return remote(part.at[c], scat.at[chip], rs_send.at[c], rs_recv.at[chip], 2 * c + core)
+
+    for step in range(blocks):
+        b = lax.rem(my_block + step + 1, blocks)
+        both = dot(cols3[...], inner_hi[b])
+        value = both[0:total] + both[total : 2 * total] + dot(cols3[0:total, :], inner_lo[b])
+        turned = value.T
+        for j in range(per_block):
+            c = b * per_block + j
+            part[c] = turned[j * own : (j + 1) * own]
+
+            @pl.when(c != chip)
+            def _():
+                rs(c).start()
+
+    local[4].wait()
+    swap[1].wait_recv()
+    span = taps * pair
+    for t in range(taps):
+        for q in range(2):
+            high, low = halves(outer[q, t])
+            at = t * pair + q * own
+            for b in range(blocks):
+                outer_all[b, at : at + own, :] = high[:, b * block : (b + 1) * block]
+                outer_all[b, span + at : span + at + own, :] = low[:, b * block : (b + 1) * block]
+
+    def rs_add(k, value):
+        source = lax.rem(chip + k, chips)
+        remote(
+            part.at[0], scat.at[source], rs_send.at[source], rs_recv.at[source], 2 * source + core
+        ).wait_recv()
+        return value + scat[source]
+
+    hidden = part[chip]
+    for k in range(1, chips):
+        hidden = rs_add(k, hidden)
+    hid[chip] = jnp.maximum(hidden, 0.0)
+
+    def ag(k):
+        to = lax.rem(chip + k, chips)
+        return remote(hid.at[chip], hid.at[chip], ag_send.at[k], ag_recv.at[chip], 2 * to + core)
+
+    def ag_start(k, carry):
+        ag(k).start()
+        return carry
+
+    lax.fori_loop(1, chips, ag_start, 0)
+
+    for step in range(blocks):
+        b = lax.rem(my_block + step, blocks)
+        for j in range(per_block):
+            source = b * per_block + j
+
+            @pl.when(source != chip)
+            def _():
+                remote(
+                    hid.at[chip], hid.at[source], ag_send.at[0], ag_recv.at[source], 2 * source + core
+                ).wait_recv()
+
+        high, low = halves(hid[pl.ds(b * per_block, per_block)].reshape(block, total))
+        both = dot(outer_all[b], high)
+        value = both[0:span] + both[span : 2 * span] + dot(outer_all[b, 0:span, :], low)
+        if step == 0:
+            taps_out[...] = value
+        else:
+            taps_out[...] += value
+
+    place = lax.broadcasted_iota(jnp.int32, (own, field_pos), 1)
+    row = lax.div(place, out_cols)
+    col = lax.rem(place, out_cols)
+
+    def shifted(q, f):
+        total_value = jnp.zeros((own, field_pos), F32)
+        for t in range(taps):
+            dr, dc = divmod(t, 3)
+            dr, dc = dr - 1, dc - 1
+            at = pl.multiple_of(t * pair + q * own, own)
+            value = taps_out[pl.ds(at, own), f * field_pos : (f + 1) * field_pos]
+            offset = dr * out_cols + dc
+            if offset:
+                value = pltpu.roll(value, (-offset) % field_pos, 1)
+                good = (row + dr >= 0) & (row + dr < wide) & (col + dc >= 0) & (col + dc < out_cols)
+                value = jnp.where(good, value, 0.0)
+            total_value = total_value + value
+        return total_value
+
+    for f in range(fields):
+        mine[:, f * field_pos : (f + 1) * field_pos] = shifted(1 - core, f)
+    last = remote(mine, theirs, fin_send.at[0], fin_recv.at[0], mate)
+    last.start()
+    kept = [shifted(core, f) for f in range(fields)]
+    last.wait_recv()
+    for f in range(fields):
+        value = (kept[f] + theirs[:, f * field_pos : (f + 1) * field_pos]).T
+        before = ext2[f, 1 : wide + 1, 8 : 8 + out_cols, :].reshape(field_pos, pair)
+        before = jnp.where(core == 0, before[:, 0:own], before[:, own:pair])
+        out_ref[f] = jnp.maximum(before + value, 0.0).reshape(wide, out_cols, own)
+
+    @pl.when(me < wide - 1)
+    def _():
+        down_copy.wait_send()
+
+    @pl.when(me > 0)
+    def _():
+        up_copy.wait_send()
+
+    for copy in swap:
+        copy.wait_send()
+
+    def a2a_done(k, carry):
+        a2a(k).wait_send()
+        return carry
+
+    lax.fori_loop(1, wide, a2a_done, 0)
+
+    def rs_done(k, carry):
+        rs(lax.rem(chip + k, chips)).wait_send()
+        ag(k).wait_send()
+        return carry
+
+    lax.fori_loop(1, chips, rs_done, 0)
+    last.wait_send()
+
+
+def fused_body(features, first_weight, down_weight, inner_weight, outer_weight):
+    wide = lax.axis_size("wide")
+    chips = wide // 2
+    fields, rows, columns, ch = features.shape
+    full = down_weight.shape[3]
+    own = full // wide
+    pair, half = 2 * own, full // 2
+    taps, quads = 9, 4
+    out_cols = columns // 2
+    total = fields * wide * out_cols
+    count, small = fields * rows * columns, fields * out_cols
+    block = 256
+    blocks = half // block
+    first = first_weight.reshape(taps, ch, ch)
+    down = down_weight.reshape(quads, ch, full)
+    inner = jnp.swapaxes(inner_weight, 3, 4).reshape(taps, own, full)
+    outer = jnp.swapaxes(outer_weight, 3, 4).reshape(taps, own, full)
+    dma = pltpu.SemaphoreType.DMA
+    return pl.pallas_call(
+        functools.partial(fused, wide),
+        out_shape=jax.ShapeDtypeStruct((fields, wide, out_cols, own), F32),
+        in_specs=[pl.BlockSpec(memory_space=pl.ANY)] * 5,
+        out_specs=pl.BlockSpec(memory_space=pltpu.VMEM),
+        scratch_shapes=[
+            pltpu.VMEM(features.shape, F32),
+            pltpu.VMEM((taps, ch, ch), F32),
+            pltpu.VMEM((quads, ch, full), F32),
+            pltpu.VMEM((2, taps, own, half), F32),
+            pltpu.VMEM((2, taps, own, half), F32),
+            pltpu.VMEM((taps * ch, ch), BF16),
+            pltpu.VMEM((taps * ch, ch), BF16),
+            pltpu.VMEM((quads * ch, full), BF16),
+            pltpu.VMEM((quads * ch, full), BF16),
+            pltpu.VMEM((blocks, taps * pair, block), BF16),
+            pltpu.VMEM((blocks, taps * pair, block), BF16),
+            pltpu.VMEM((blocks, 2 * taps * pair, block), BF16),
+            pltpu.VMEM((2, fields, columns, ch), F32),
+            pltpu.VMEM((fields, rows + 2, columns + 16, ch), F32),
+            pltpu.VMEM((2 * count, taps * ch), BF16),
+            pltpu.VMEM((ch // 128, count, 128), F32),
+            pltpu.VMEM((2 * small, quads * ch), BF16),
+            pltpu.VMEM((chips, small, pair), F32),
+            pltpu.VMEM((wide, small, pair), F32),
+            pltpu.VMEM((fields, wide + 2, out_cols + 16, pair), F32),
+            pltpu.VMEM((2 * total, taps * pair), BF16),
+            pltpu.VMEM((chips, own, total), F32),
+            pltpu.VMEM((chips, own, total), F32),
+            pltpu.VMEM((chips, own, total), F32),
+            pltpu.VMEM((taps * pair, total), F32),
+            pltpu.VMEM((own, total), F32),
+            pltpu.VMEM((own, total), F32),
+            dma((5,)), dma((2,)), dma((2,)), dma((2,)), dma((2,)),
+            dma((wide,)), dma((wide,)), dma((chips,)), dma((chips,)), dma((chips,)), dma((chips,)),
+            dma((1,)), dma((1,)),
+        ],
+        compiler_params=pltpu.CompilerParams(
+            collective_id=0, has_side_effects=True, vmem_limit_bytes=48 << 20
+        ),
+        cost_estimate=pl.CostEstimate(
+            flops=2 * total * taps * full * full // chips, bytes_accessed=12 << 20, transcendentals=0
+        ),
+    )(features, first, down, inner, outer)
+
+
+def fits(features, first_weight, down_weight, inner_weight):
+    wide = lax.axis_size("wide")
+    fields, rows, columns, ch = features.shape
+    full = down_weight.shape[3]
+    own = full // wide
+    return (
+        wide % 2 == 0 and rows == 2 and inner_weight.shape[0] == 1 and own % 64 == 0
+        and 256 % own == 0 and full % 512 == 0 and ch % 128 == 0 and columns == 16
+        and (wide * columns // 2) % 128 == 0 and fields * wide * columns <= 1024
+    )
+
+
+def choose(features, first_weight, down_weight, inner_weight, outer_weight):
+    whole = fused_body if fits(features, first_weight, down_weight, inner_weight) else body
+    return whole(features, first_weight, down_weight, inner_weight, outer_weight)
+
 
 def solution(mesh):
     in_specs = (
@@ -118,4 +512,4 @@
         P(None, None, None, None, "wide"),
     )
     out_specs = P("groups", None, None, "wide")
-    return jax.shard_map(body, mesh=mesh, in_specs=in_specs, out_specs=out_specs, check_vma=False)
+    return jax.shard_map(choose, mesh=mesh, in_specs=in_specs, out_specs=out_specs, check_vma=False)

time: 162 us -> 48.1 us (0.30)
  the two profiles are of different devices: /device:TPU:1 before, /device:TPU:25 now
where the time goes in v1:
time: 48.1 us; the launch traced here: 47.9 us
  Pallas kernels  43 us (89%)
  local copies, waits for them, and re-layouts  4.83 us (10%)
    pallas_call x1, Pallas kernels, fused_body(): pl.pallas_call(functools.partial(fused, wide), out_shape=jax.ShapeDtypeSt...  43 us
    unnamed x7, local copies, waits for them, and re-layouts  4.83 us

profile of v1, /device:TPU:25, one launch (start us, length us, event | category | flops | bytes accessed | tf_op | source)
XLA Modules:
  0.0 47.9 jit_solution(8091726159996475940)
XLA Ops:
  0.0 0.0 copy-start
  0.0 1.7 %copy-done = f32[3,3,256,256]{3,2,1,0:T(8,128)S(1)} copy-done((f32[3,3,256,256]{3,2,1,0:T(8,128)S(1)}, f32[3,3,256,256]{3,2,1,0:T(8,128)}, u32[]{:S(2)}) %copy-start) | copy-done | bytes 2359320
  1.7 0.0 copy-start.1
  1.7 1.7 %copy-done.1 = f32[1,3,3,1024,64]{3,4,2,1,0:T(8,128)S(1)} copy-done((f32[1,3,3,1024,64]{3,4,2,1,0:T(8,128)S(1)}, f32[1,3,3,1024,64]{3,4,2,1,0:T(8,128)}, u32[]{:S(2)}) %copy-start.1) | copy-done | bytes 2359320
  3.3 0.0 copy-start.2
  3.3 0.8 %copy-done.2 = f32[2,2,16,256]{3,2,1,0:T(8,128)S(1)} copy-done((f32[2,2,16,256]{3,2,1,0:T(8,128)S(1)}, f32[2,2,16,256]{3,2,1,0:T(8,128)}, u32[]{:S(2)}) %copy-start.2) | copy-done | bytes 65560
  4.2 43.0 %shard_map.55 = f32[2,16,8,64]{3,2,1,0:T(8,128)S(1)} custom-call(f32[2,2,16,256]{3,2,1,0:T(8,128)S(1)} %copy-done.2, f32[9,256,256]{2,1,0:T(8,128)S(1)} %bitcast.8, f32[4,256,1024]{2,1,0:T(8,128)} %bitcast.10, f32[9,64,1024]{2,1,0:T(8,128)S(1)} %bitcast.9, f32[9,64,1024]{2,1,0:T(8,128)} %bitcast.11), custom_call_target="tpu_custom_call" | custom-call | flops 603979776 | bytes 12582912 | tf_op jit(solution)/shard_map/pallas_call | solution.py:443
  47.2 0.7 %copy.7 = f32[2,16,8,64]{3,2,1,0:T(8,128)} copy(f32[2,16,8,64]{3,2,1,0:T(8,128)S(1)} %shard_map.55) | data formatting | bytes 131072
Async XLA Ops:
  0.0 1.7 %copy-start = (f32[3,3,256,256]{3,2,1,0:T(8,128)S(1)}, f32[3,3,256,256]{3,2,1,0:T(8,128)}, u32[]{:S(2)}) copy-start(f32[3,3,256,256]{3,2,1,0:T(8,128)} %param.6) | copy-start | bytes 7077892
  1.7 1.7 %copy-start.1 = (f32[1,3,3,1024,64]{3,4,2,1,0:T(8,128)S(1)}, f32[1,3,3,1024,64]{3,4,2,1,0:T(8,128)}, u32[]{:S(2)}) copy-start(f32[1,3,3,1024,64]{3,4,2,1,0:T(8,128)} %param.8) | copy-start | bytes 7077892
  3.3 0.8 %copy-start.2 = (f32[2,2,16,256]{3,2,1,0:T(8,128)S(1)}, f32[2,2,16,256]{3,2,1,0:T(8,128)}, u32[]{:S(2)}) copy-start(f32[2,2,16,256]{3,2,1,0:T(8,128)} %feat_hbm.1) | copy-start | bytes 196612

commit v2 on v1

--- a/solution.py
+++ b/solution.py
@@ -132,15 +132,21 @@
     feat, first, down, inner, outer,
     first_hi, first_lo, down_hi, down_lo, inner_hi, inner_lo, outer_all,
     halo, ext, cols1, act, cols2, red, gathered, ext2, cols3,
-    part, scat, hid, taps_out, mine, theirs,
+    part, from_y, to_z, from_z, hid, taps_out, mine, theirs,
     local_sem, halo_send, halo_recv, weight_send, weight_recv,
-    a2a_send, a2a_recv, rs_send, rs_recv, ag_send, ag_recv, fin_send, fin_recv,
+    a2a_send, a2a_recv, rsy_send, rsy_recv, rsz_send, rsz_recv, agy_send, agz_send, ag_recv,
+    fin_send, fin_recv, relay, known,
 ):
     me = lax.axis_index("wide")
     core = lax.rem(me, 2)
     chip = lax.div(me, 2)
     mate = me + 1 - 2 * core
     chips = wide // 2
+    line = chips // 2
+    z = lax.div(chip, 2)
+    y = lax.rem(chip, 2)
+    across = me + 2 - 4 * y
+    beside = me - 1 + 2 * core
     fields, rows, columns, ch = feat.shape
     own = inner.shape[2]
     half = inner.shape[3]
@@ -170,18 +176,55 @@
         copy.start()
 
     barrier = pltpu.get_barrier_semaphore()
-
-    def greet(k, carry):
+    has_below = z > 0
+    has_above = z < line - 1
+    has_beside = (beside >= 0) & (beside < wide)
+
+    def signal(semaphore, device):
         pl.semaphore_signal(
-            barrier, inc=1, device_id={"wide": lax.rem(me + k, wide)}, device_id_type=MESH
+            semaphore, inc=1, device_id={"wide": device}, device_id_type=MESH
         )
-        return carry
-
-    lax.fori_loop(1, wide, greet, 0)
+
+    signal(barrier, mate)
+    signal(barrier, across)
+
+    @pl.when(has_beside)
+    def _():
+        signal(barrier, beside)
+
+    @pl.when(has_below)
+    def _():
+        signal(barrier, me - 4)
+
+    @pl.when(has_above)
+    def _():
+        signal(barrier, me + 4)
+
+    def relay_tell(r):
+        @pl.when(has_above)
+        def _():
+            signal(relay.at[2 * r], me + 4)
+
+        @pl.when(has_below)
+        def _():
+            signal(relay.at[2 * r + 1], me - 4)
+
+    def relay_hear(r):
+        @pl.when(has_below)
+        def _():
+            pl.semaphore_wait(relay.at[2 * r], 1)
+
+        @pl.when(has_above)
+        def _():
+            pl.semaphore_wait(relay.at[2 * r + 1], 1)
+
     ext[...] = jnp.zeros_like(ext)
     ext2[...] = jnp.zeros_like(ext2)
     local[0].wait()
-    pl.semaphore_wait(barrier, wide - 1)
+    greeted = (
+        2 + has_beside.astype(jnp.int32) + has_below.astype(jnp.int32) + has_above.astype(jnp.int32)
+    )
+    pl.semaphore_wait(barrier, greeted)
 
     down_copy = remote(feat.at[:, rows - 1], halo.at[0], halo_send.at[0], halo_recv.at[0], me + 1)
     up_copy = remote(feat.at[:, 0], halo.at[1], halo_send.at[1], halo_recv.at[1], me - 1)
@@ -201,6 +244,15 @@
     for copy in swap:
         copy.start()
 
+    def prepare_down():
+        for t in range(down.shape[0]):
+            high, low = halves(down[t])
+            down_hi[t * ch : (t + 1) * ch, :] = high
+            down_lo[t * ch : (t + 1) * ch, :] = low
+
+    rounds = line - 2
+    if rounds:
+        relay_tell(0)
     ext[:, 1 : rows + 1, 8 : 8 + columns, :] = feat[...]
     local[1].wait()
     taps = first.shape[0]
@@ -208,11 +260,17 @@
         high, low = halves(first[t])
         first_hi[t * ch : (t + 1) * ch, :] = high
         first_lo[t * ch : (t + 1) * ch, :] = low
-    local[2].wait()
-    for t in range(down.shape[0]):
-        high, low = halves(down[t])
-        down_hi[t * ch : (t + 1) * ch, :] = high
-        down_lo[t * ch : (t + 1) * ch, :] = low
+    for r in range(rounds):
+        relay_hear(r)
+        if r + 1 < rounds:
+            relay_tell(r + 1)
+        if r == 0:
+            local[2].wait()
+            prepare_down()
+    if not rounds:
+        local[2].wait()
+        prepare_down()
+    signal(known.at[0], across)
 
     @pl.when(me > 0)
     def _():
@@ -224,6 +282,8 @@
         up_copy.wait_recv()
         ext[:, rows + 1, 8 : 8 + columns, :] = halo[1]
 
+    pl.semaphore_wait(known.at[0], 1)
+    signal(known.at[1], mate)
     count = fields * rows * columns
     for t in range(taps):
         dr, dc = divmod(t, 3)
@@ -265,6 +325,7 @@
         a2a(k).start()
         return carry
 
+    pl.semaphore_wait(known.at[1], 1)
     lax.fori_loop(1, wide, a2a_start, 0)
     gathered[me] = red[chip]
 
@@ -297,8 +358,17 @@
 
     my_block = lax.div(chip, per_block)
 
-    def rs(c):
-        return remote(part.at[c], scat.at[chip], rs_send.at[c], rs_recv.at[chip], 2 * c + core)
+    half_block = per_block // 2
+
+    def rs_y(zz):
+        return remote(
+            part.at[2 * zz + 1 - y], from_y.at[zz], rsy_send.at[zz], rsy_recv.at[zz], across
+        )
+
+    def rs_z(zz):
+        return remote(
+            to_z.at[zz], from_z.at[z], rsz_send.at[zz], rsz_recv.at[z], 4 * zz + 2 * y + core
+        )
 
     for step in range(blocks):
         b = lax.rem(my_block + step + 1, blocks)
@@ -306,12 +376,20 @@
         value = both[0:total] + both[total : 2 * total] + dot(cols3[0:total, :], inner_lo[b])
         turned = value.T
         for j in range(per_block):
-            c = b * per_block + j
-            part[c] = turned[j * own : (j + 1) * own]
-
-            @pl.when(c != chip)
+            part[b * per_block + j] = turned[j * own : (j + 1) * own]
+        for j in range(half_block):
+            rs_y(b * half_block + j).start()
+
+    for step in range(blocks):
+        b = lax.rem(my_block + step + 1, blocks)
+        for j in range(half_block):
+            zz = b * half_block + j
+            rs_y(zz).wait_recv()
+            to_z[zz] = part[2 * zz + y] + from_y[zz]
+
+            @pl.when(zz != z)
             def _():
-                rs(c).start()
+                rs_z(zz).start()
 
     local[4].wait()
     swap[1].wait_recv()
@@ -324,38 +402,50 @@
                 outer_all[b, at : at + own, :] = high[:, b * block : (b + 1) * block]
                 outer_all[b, span + at : span + at + own, :] = low[:, b * block : (b + 1) * block]
 
-    def rs_add(k, value):
-        source = lax.rem(chip + k, chips)
+    hidden = to_z[z]
+    for k in range(1, line):
+        source = lax.rem(z + k, line)
         remote(
-            part.at[0], scat.at[source], rs_send.at[source], rs_recv.at[source], 2 * source + core
+            to_z.at[0], from_z.at[source], rsz_send.at[source], rsz_recv.at[source],
+            4 * source + 2 * y + core,
         ).wait_recv()
-        return value + scat[source]
-
-    hidden = part[chip]
-    for k in range(1, chips):
-        hidden = rs_add(k, hidden)
+        hidden = hidden + from_z[source]
     hid[chip] = jnp.maximum(hidden, 0.0)
 
-    def ag(k):
-        to = lax.rem(chip + k, chips)
-        return remote(hid.at[chip], hid.at[chip], ag_send.at[k], ag_recv.at[chip], 2 * to + core)
-
-    def ag_start(k, carry):
-        ag(k).start()
-        return carry
-
-    lax.fori_loop(1, chips, ag_start, 0)
-
+    def ag_z(zz):
+        return remote(
+            hid.at[chip], hid.at[chip], agz_send.at[zz], ag_recv.at[chip], 4 * zz + 2 * y + core
+        )
+
+    def ag_y(zz):
+        c = 2 * zz + y
+        return remote(hid.at[c], hid.at[c], agy_send.at[zz], ag_recv.at[c], across)
+
+    def arrived(c, device):
+        remote(hid.at[chip], hid.at[c], agz_send.at[0], ag_recv.at[c], device).wait_recv()
+
+    for step in range(blocks):
+        b = lax.rem(my_block + step + 1, blocks)
+        for j in range(half_block):
+            zz = b * half_block + j
+
+            @pl.when(zz != z)
+            def _():
+                ag_z(zz).start()
+
+    ag_y(z).start()
     for step in range(blocks):
         b = lax.rem(my_block + step, blocks)
-        for j in range(per_block):
-            source = b * per_block + j
-
-            @pl.when(source != chip)
+        for j in range(half_block):
+            zz = b * half_block + j
+
+            @pl.when(zz != z)
             def _():
-                remote(
-                    hid.at[chip], hid.at[source], ag_send.at[0], ag_recv.at[source], 2 * source + core
-                ).wait_recv()
+                arrived(2 * zz + y, 4 * zz + 2 * y + core)
+                ag_y(zz).start()
+
+        for j in range(half_block):
+            arrived(2 * (b * half_block + j) + 1 - y, across)
 
         high, low = halves(hid[pl.ds(b * per_block, per_block)].reshape(block, total))
         both = dot(outer_all[b], high)
@@ -413,12 +503,15 @@
 
     lax.fori_loop(1, wide, a2a_done, 0)
 
-    def rs_done(k, carry):
-        rs(lax.rem(chip + k, chips)).wait_send()
-        ag(k).wait_send()
-        return carry
-
-    lax.fori_loop(1, chips, rs_done, 0)
+    for zz in range(line):
+        rs_y(zz).wait_send()
+        ag_y(zz).wait_send()
+
+        @pl.when(zz != z)
+        def _():
+            rs_z(zz).wait_send()
+            ag_z(zz).wait_send()
+
     last.wait_send()
 
 
@@ -468,17 +561,21 @@
             pltpu.VMEM((fields, wide + 2, out_cols + 16, pair), F32),
             pltpu.VMEM((2 * total, taps * pair), BF16),
             pltpu.VMEM((chips, own, total), F32),
-            pltpu.VMEM((chips, own, total), F32),
+            pltpu.VMEM((chips // 2, own, total), F32),
+            pltpu.VMEM((chips // 2, own, total), F32),
+            pltpu.VMEM((chips // 2, own, total), F32),
             pltpu.VMEM((chips, own, total), F32),
             pltpu.VMEM((taps * pair, total), F32),
             pltpu.VMEM((own, total), F32),
             pltpu.VMEM((own, total), F32),
             dma((5,)), dma((2,)), dma((2,)), dma((2,)), dma((2,)),
-            dma((wide,)), dma((wide,)), dma((chips,)), dma((chips,)), dma((chips,)), dma((chips,)),
+            dma((wide,)), dma((wide,)), dma((chips // 2,)), dma((chips // 2,)), dma((chips // 2,)),
+            dma((chips // 2,)), dma((chips // 2,)), dma((chips // 2,)), dma((chips,)),
             dma((1,)), dma((1,)),
+            pltpu.SemaphoreType.REGULAR((max(2, chips - 4),)), pltpu.SemaphoreType.REGULAR((2,)),
         ],
         compiler_params=pltpu.CompilerParams(
-            collective_id=0, has_side_effects=True, vmem_limit_bytes=48 << 20
+            collective_id=0, has_side_effects=True, vmem_limit_bytes=62 << 20
         ),
         cost_estimate=pl.CostEstimate(
             flops=2 * total * taps * full * full // chips, bytes_accessed=12 << 20, transcendentals=0
@@ -492,8 +589,8 @@
     full = down_weight.shape[3]
     own = full // wide
     return (
-        wide % 2 == 0 and rows == 2 and inner_weight.shape[0] == 1 and own % 64 == 0
-        and 256 % own == 0 and full % 512 == 0 and ch % 128 == 0 and columns == 16
+        wide % 8 == 0 and rows == 2 and inner_weight.shape[0] == 1 and own % 64 == 0
+        and 128 % own == 0 and full % 512 == 0 and ch % 128 == 0 and columns == 16
         and (wide * columns // 2) % 128 == 0 and fields * wide * columns <= 1024
     )
 

time: 48.1 us -> 44.8 us (0.931)
  the two profiles are of different devices: /device:TPU:25 before, /device:TPU:1 now
where the time goes in v2:
time: 44.8 us; the launch traced here: 43.9 us
  Pallas kernels  42.4 us (95%)
  local copies, waits for them, and re-layouts  1.57 us (4%)
    pallas_call x1, Pallas kernels, fused_body(): pl.pallas_call(functools.partial(fused, wide), out_shape=jax.ShapeDtypeSt...  42.4 us
    unnamed x1, local copies, waits for them, and re-layouts  1.57 us

profile of v2, /device:TPU:1, one launch (start us, length us, event | category | flops | bytes accessed | tf_op | source)
XLA Modules:
  0.0 43.9 jit_solution(11727238031274110622)
XLA Ops:
  0.0 42.4 %shard_map.55 = f32[2,16,8,64]{3,2,1,0:T(8,128)} custom-call(f32[2,2,16,256]{3,2,1,0:T(8,128)} %feat_hbm.1, f32[9,256,256]{2,1,0:T(8,128)} %bitcast.9, f32[4,256,1024]{2,1,0:T(8,128)} %bitcast.8, f32[9,64,1024]{2,1,0:T(8,128)} %bitcast.10, f32[9,64,1024]{2,1,0:T(8,128)} %bitcast.11), custom_call_target="tpu_custom_call" | custom-call | flops 603979776 | bytes 12582912 | tf_op jit(solution)/shard_map/pallas_call | solution.py:536
  42.4 1.6 %copy.7 = f32[2,16,8,64]{3,2,1,0:T(8,128)} copy(f32[2,16,8,64]{3,2,1,0:T(8,128)} %shard_map.55) | data formatting | bytes 131072

commit v3 on v2

--- a/solution.py
+++ b/solution.py
@@ -348,48 +348,50 @@
 
     for f in range(fields):
         ext2[f, 1 : wide + 1, 8 : 8 + out_cols, :] = gathered[:, f * out_cols : (f + 1) * out_cols, :]
-    total = fields * field_pos
-    for t in range(taps):
-        dr, dc = divmod(t, 3)
-        slab = ext2[:, dr : dr + wide, 7 + dc : 7 + dc + out_cols, :].reshape(total, pair)
-        high, low = halves(slab)
-        cols3[0:total, t * pair : (t + 1) * pair] = high
-        cols3[total : 2 * total, t * pair : (t + 1) * pair] = low
-
     my_block = lax.div(chip, per_block)
-
     half_block = per_block // 2
 
-    def rs_y(zz):
+    def rs_y(f, zz):
+        at = f * line + zz
         return remote(
-            part.at[2 * zz + 1 - y], from_y.at[zz], rsy_send.at[zz], rsy_recv.at[zz], across
+            part.at[f * chips + 2 * zz + 1 - y], from_y.at[at], rsy_send.at[at], rsy_recv.at[at], across
         )
 
-    def rs_z(zz):
+    def rs_z(f, zz):
+        at = f * line
         return remote(
-            to_z.at[zz], from_z.at[z], rsz_send.at[zz], rsz_recv.at[z], 4 * zz + 2 * y + core
+            to_z.at[at + zz], from_z.at[at + z], rsz_send.at[at + zz], rsz_recv.at[at + z],
+            4 * zz + 2 * y + core,
         )
 
-    for step in range(blocks):
-        b = lax.rem(my_block + step + 1, blocks)
-        both = dot(cols3[...], inner_hi[b])
-        value = both[0:total] + both[total : 2 * total] + dot(cols3[0:total, :], inner_lo[b])
-        turned = value.T
-        for j in range(per_block):
-            part[b * per_block + j] = turned[j * own : (j + 1) * own]
-        for j in range(half_block):
-            rs_y(b * half_block + j).start()
-
-    for step in range(blocks):
-        b = lax.rem(my_block + step + 1, blocks)
-        for j in range(half_block):
-            zz = b * half_block + j
-            rs_y(zz).wait_recv()
-            to_z[zz] = part[2 * zz + y] + from_y[zz]
-
-            @pl.when(zz != z)
-            def _():
-                rs_z(zz).start()
+    for f in range(fields):
+        for t in range(taps):
+            dr, dc = divmod(t, 3)
+            slab = ext2[f, dr : dr + wide, 7 + dc : 7 + dc + out_cols, :].reshape(field_pos, pair)
+            high, low = halves(slab)
+            cols3[f, 0:field_pos, t * pair : (t + 1) * pair] = high
+            cols3[f, field_pos : 2 * field_pos, t * pair : (t + 1) * pair] = low
+        for step in range(blocks):
+            b = lax.rem(my_block + step + 1, blocks)
+            both = dot(cols3[f], inner_hi[b])
+            value = both[0:field_pos] + both[field_pos:] + dot(cols3[f, 0:field_pos, :], inner_lo[b])
+            turned = value.T
+            for j in range(per_block):
+                part[f * chips + b * per_block + j] = turned[j * own : (j + 1) * own]
+            for j in range(half_block):
+                rs_y(f, b * half_block + j).start()
+
+    def pass_on(f):
+        for step in range(blocks):
+            b = lax.rem(my_block + step + 1, blocks)
+            for j in range(half_block):
+                zz = b * half_block + j
+                rs_y(f, zz).wait_recv()
+                to_z[f * line + zz] = part[f * chips + 2 * zz + y] + from_y[f * line + zz]
+
+                @pl.when(zz != z)
+                def _():
+                    rs_z(f, zz).start()
 
     local[4].wait()
     swap[1].wait_recv()
@@ -402,58 +404,66 @@
                 outer_all[b, at : at + own, :] = high[:, b * block : (b + 1) * block]
                 outer_all[b, span + at : span + at + own, :] = low[:, b * block : (b + 1) * block]
 
-    hidden = to_z[z]
-    for k in range(1, line):
-        source = lax.rem(z + k, line)
-        remote(
-            to_z.at[0], from_z.at[source], rsz_send.at[source], rsz_recv.at[source],
-            4 * source + 2 * y + core,
-        ).wait_recv()
-        hidden = hidden + from_z[source]
-    hid[chip] = jnp.maximum(hidden, 0.0)
-
-    def ag_z(zz):
+    for f in range(fields):
+        pass_on(f)
+
+    def ag_z(f, zz):
+        at = f * chips + chip
         return remote(
-            hid.at[chip], hid.at[chip], agz_send.at[zz], ag_recv.at[chip], 4 * zz + 2 * y + core
+            hid.at[at], hid.at[at], agz_send.at[f * line + zz], ag_recv.at[at], 4 * zz + 2 * y + core
         )
 
-    def ag_y(zz):
-        c = 2 * zz + y
-        return remote(hid.at[c], hid.at[c], agy_send.at[zz], ag_recv.at[c], across)
-
-    def arrived(c, device):
-        remote(hid.at[chip], hid.at[c], agz_send.at[0], ag_recv.at[c], device).wait_recv()
-
-    for step in range(blocks):
-        b = lax.rem(my_block + step + 1, blocks)
-        for j in range(half_block):
-            zz = b * half_block + j
-
-            @pl.when(zz != z)
-            def _():
-                ag_z(zz).start()
-
-    ag_y(z).start()
-    for step in range(blocks):
+    def ag_y(f, zz):
+        at = f * chips + 2 * zz + y
+        return remote(hid.at[at], hid.at[at], agy_send.at[f * line + zz], ag_recv.at[at], across)
+
+    def arrived(f, c, device):
+        at = f * chips + c
+        remote(hid.at[at], hid.at[at], agz_send.at[0], ag_recv.at[at], device).wait_recv()
+
+    def collect(f):
+        hidden = to_z[f * line + z]
+        for k in range(1, line):
+            source = lax.rem(z + k, line)
+            at = f * line + source
+            remote(
+                to_z.at[0], from_z.at[at], rsz_send.at[at], rsz_recv.at[at], 4 * source + 2 * y + core
+            ).wait_recv()
+            hidden = hidden + from_z[at]
+        hid[f * chips + chip] = jnp.maximum(hidden, 0.0)
+        for step in range(blocks):
+            b = lax.rem(my_block + step + 1, blocks)
+            for j in range(half_block):
+                zz = b * half_block + j
+
+                @pl.when(zz != z)
+                def _():
+                    ag_z(f, zz).start()
+
+        ag_y(f, z).start()
+
+    def forward(f, step):
         b = lax.rem(my_block + step, blocks)
         for j in range(half_block):
             zz = b * half_block + j
 
             @pl.when(zz != z)
             def _():
-                arrived(2 * zz + y, 4 * zz + 2 * y + core)
-                ag_y(zz).start()
-
+                arrived(f, 2 * zz + y, 4 * zz + 2 * y + core)
+                ag_y(f, zz).start()
+
+    def multiply(f, step):
+        b = lax.rem(my_block + step, blocks)
         for j in range(half_block):
-            arrived(2 * (b * half_block + j) + 1 - y, across)
-
-        high, low = halves(hid[pl.ds(b * per_block, per_block)].reshape(block, total))
+            arrived(f, 2 * (b * half_block + j) + 1 - y, across)
+        gained = hid[pl.ds(f * chips + b * per_block, per_block)].reshape(block, field_pos)
+        high, low = halves(gained)
         both = dot(outer_all[b], high)
         value = both[0:span] + both[span : 2 * span] + dot(outer_all[b, 0:span, :], low)
         if step == 0:
-            taps_out[...] = value
+            taps_out[f] = value
         else:
-            taps_out[...] += value
+            taps_out[f] += value
 
     place = lax.broadcasted_iota(jnp.int32, (own, field_pos), 1)
     row = lax.div(place, out_cols)
@@ -465,7 +475,7 @@
             dr, dc = divmod(t, 3)
             dr, dc = dr - 1, dc - 1
             at = pl.multiple_of(t * pair + q * own, own)
-            value = taps_out[pl.ds(at, own), f * field_pos : (f + 1) * field_pos]
+            value = taps_out[f, pl.ds(at, own), :]
             offset = dr * out_cols + dc
             if offset:
                 value = pltpu.roll(value, (-offset) % field_pos, 1)
@@ -474,14 +484,27 @@
             total_value = total_value + value
         return total_value
 
+    def last(f):
+        return remote(mine.at[f], theirs.at[f], fin_send.at[f], fin_recv.at[f], mate)
+
+    def give(f):
+        mine[f] = shifted(1 - core, f)
+        last(f).start()
+
     for f in range(fields):
-        mine[:, f * field_pos : (f + 1) * field_pos] = shifted(1 - core, f)
-    last = remote(mine, theirs, fin_send.at[0], fin_recv.at[0], mate)
-    last.start()
-    kept = [shifted(core, f) for f in range(fields)]
-    last.wait_recv()
+        collect(f)
+    for step in range(blocks):
+        forward(0, step)
     for f in range(fields):
-        value = (kept[f] + theirs[:, f * field_pos : (f + 1) * field_pos]).T
+        for step in range(blocks):
+            multiply(f, step)
+            if f + 1 < fields:
+                forward(f + 1, step)
+        give(f)
+    for f in range(fields):
+        kept = shifted(core, f)
+        last(f).wait_recv()
+        value = (kept + theirs[f]).T
         before = ext2[f, 1 : wide + 1, 8 : 8 + out_cols, :].reshape(field_pos, pair)
         before = jnp.where(core == 0, before[:, 0:own], before[:, own:pair])
         out_ref[f] = jnp.maximum(before + value, 0.0).reshape(wide, out_cols, own)
@@ -503,16 +526,16 @@
 
     lax.fori_loop(1, wide, a2a_done, 0)
 
-    for zz in range(line):
-        rs_y(zz).wait_send()
-        ag_y(zz).wait_send()
-
-        @pl.when(zz != z)
-        def _():
-            rs_z(zz).wait_send()
-            ag_z(zz).wait_send()
-
-    last.wait_send()
+    for f in range(fields):
+        last(f).wait_send()
+        for zz in range(line):
+            rs_y(f, zz).wait_send()
+            ag_y(f, zz).wait_send()
+
+            @pl.when(zz != z)
+            def _():
+                rs_z(f, zz).wait_send()
+                ag_z(f, zz).wait_send()
 
 
 def fused_body(features, first_weight, down_weight, inner_weight, outer_weight):
@@ -524,7 +547,8 @@
     pair, half = 2 * own, full // 2
     taps, quads = 9, 4
     out_cols = columns // 2
-    total = fields * wide * out_cols
+    place, line = wide * out_cols, chips // 2
+    total = fields * place
     count, small = fields * rows * columns, fields * out_cols
     block = 256
     blocks = half // block
@@ -559,19 +583,19 @@
             pltpu.VMEM((chips, small, pair), F32),
             pltpu.VMEM((wide, small, pair), F32),
             pltpu.VMEM((fields, wide + 2, out_cols + 16, pair), F32),
-            pltpu.VMEM((2 * total, taps * pair), BF16),
-            pltpu.VMEM((chips, own, total), F32),
-            pltpu.VMEM((chips // 2, own, total), F32),
-            pltpu.VMEM((chips // 2, own, total), F32),
-            pltpu.VMEM((chips // 2, own, total), F32),
-            pltpu.VMEM((chips, own, total), F32),
-            pltpu.VMEM((taps * pair, total), F32),
-            pltpu.VMEM((own, total), F32),
-            pltpu.VMEM((own, total), F32),
+            pltpu.VMEM((fields, 2 * place, taps * pair), BF16),
+            pltpu.VMEM((fields * chips, own, place), F32),
+            pltpu.VMEM((fields * line, own, place), F32),
+            pltpu.VMEM((fields * line, own, place), F32),
+            pltpu.VMEM((fields * line, own, place), F32),
+            pltpu.VMEM((fields * chips, own, place), F32),
+            pltpu.VMEM((fields, taps * pair, place), F32),
+            pltpu.VMEM((fields, own, place), F32),
+            pltpu.VMEM((fields, own, place), F32),
             dma((5,)), dma((2,)), dma((2,)), dma((2,)), dma((2,)),
-            dma((wide,)), dma((wide,)), dma((chips // 2,)), dma((chips // 2,)), dma((chips // 2,)),
-            dma((chips // 2,)), dma((chips // 2,)), dma((chips // 2,)), dma((chips,)),
-            dma((1,)), dma((1,)),
+            dma((wide,)), dma((wide,)), dma((fields * line,)), dma((fields * line,)),
+            dma((fields * line,)), dma((fields * line,)), dma((fields * line,)), dma((fields * line,)),
+            dma((fields * chips,)), dma((fields,)), dma((fields,)),
             pltpu.SemaphoreType.REGULAR((max(2, chips - 4),)), pltpu.SemaphoreType.REGULAR((2,)),
         ],
         compiler_params=pltpu.CompilerParams(

time: 44.8 us -> 42.5 us (0.949); the launches traced: 43.9 us -> 42.3 us
  Pallas kernels: 42.4 us -> 40.7 us
    pallas_call x1, Pallas kernels: 42.4 us -> 40.7 us  [fused_body(): pl.pallas_call(functools.partial(fused, wide), out_shape=jax.ShapeDtypeSt...]
where the time goes in v3:
time: 42.5 us; the launch traced here: 42.3 us
  Pallas kernels  40.7 us (96%)
  local copies, waits for them, and re-layouts  1.57 us (4%)
    pallas_call x1, Pallas kernels, fused_body(): pl.pallas_call(functools.partial(fused, wide), out_shape=jax.ShapeDtypeSt...  40.7 us
    unnamed x1, local copies, waits for them, and re-layouts  1.57 us

profile of v3, /device:TPU:1, one launch (start us, length us, event | category | flops | bytes accessed | tf_op | source)
XLA Modules:
  0.0 42.3 jit_solution(2541904474973605588)
XLA Ops:
  0.0 40.7 %shard_map.55 = f32[2,16,8,64]{3,2,1,0:T(8,128)} custom-call(f32[2,2,16,256]{3,2,1,0:T(8,128)} %feat_hbm.1, f32[9,256,256]{2,1,0:T(8,128)} %bitcast.9, f32[4,256,1024]{2,1,0:T(8,128)} %bitcast.8, f32[9,64,1024]{2,1,0:T(8,128)} %bitcast.10, f32[9,64,1024]{2,1,0:T(8,128)} %bitcast.11), custom_call_target="tpu_custom_call" | custom-call | flops 603979776 | bytes 12582912 | tf_op jit(solution)/shard_map/pallas_call | solution.py:560
  40.8 1.6 %copy.7 = f32[2,16,8,64]{3,2,1,0:T(8,128)} copy(f32[2,16,8,64]{3,2,1,0:T(8,128)} %shard_map.55) | data formatting | bytes 131072

commit v4 on v3

--- a/solution.py
+++ b/solution.py
@@ -322,7 +322,7 @@
         return remote(red.at[lax.div(to, 2)], gathered.at[me], a2a_send.at[k], a2a_recv.at[me], to)
 
     def a2a_start(k, carry):
-        a2a(k).start()
+        a2a(1 + lax.rem(k + wide // 2 - 3, wide - 1)).start()
         return carry
 
     pl.semaphore_wait(known.at[1], 1)
@@ -338,6 +338,17 @@
             for b in range(blocks):
                 inner_hi[b, at : at + own, :] = high[:, b * block : (b + 1) * block]
                 inner_lo[b, at : at + own, :] = low[:, b * block : (b + 1) * block]
+
+    local[4].wait()
+    swap[1].wait_recv()
+    span = taps * pair
+    for t in range(taps):
+        for q in range(2):
+            high, low = halves(outer[q, t])
+            at = t * pair + q * own
+            for b in range(blocks):
+                outer_all[b, at : at + own, :] = high[:, b * block : (b + 1) * block]
+                outer_all[b, span + at : span + at + own, :] = low[:, b * block : (b + 1) * block]
 
     def a2a_wait(k, carry):
         source = lax.rem(me + k, wide)
@@ -392,17 +403,6 @@
                 @pl.when(zz != z)
                 def _():
                     rs_z(f, zz).start()
-
-    local[4].wait()
-    swap[1].wait_recv()
-    span = taps * pair
-    for t in range(taps):
-        for q in range(2):
-            high, low = halves(outer[q, t])
-            at = t * pair + q * own
-            for b in range(blocks):
-                outer_all[b, at : at + own, :] = high[:, b * block : (b + 1) * block]
-                outer_all[b, span + at : span + at + own, :] = low[:, b * block : (b + 1) * block]
 
     for f in range(fields):
         pass_on(f)

time: 42.5 us -> 41.9 us (0.986)
  Pallas kernels: 40.7 us -> 40.2 us
    pallas_call x1, Pallas kernels: 40.7 us -> 40.2 us  [fused_body(): pl.pallas_call(functools.partial(fused, wide), out_shape=jax.ShapeDtypeSt...]
where the time goes in v4:
time: 41.9 us; the launch traced here: 41.7 us
  Pallas kernels  40.2 us (96%)
  local copies, waits for them, and re-layouts  1.57 us (4%)
    pallas_call x1, Pallas kernels, fused_body(): pl.pallas_call(functools.partial(fused, wide), out_shape=jax.ShapeDtypeSt...  40.2 us
    unnamed x1, local copies, waits for them, and re-layouts  1.57 us

profile of v4, /device:TPU:1, one launch (start us, length us, event | category | flops | bytes accessed | tf_op | source)
XLA Modules:
  0.0 41.7 jit_solution(16457531480225073135)
XLA Ops:
  0.0 40.2 %shard_map.55 = f32[2,16,8,64]{3,2,1,0:T(8,128)} custom-call(f32[2,2,16,256]{3,2,1,0:T(8,128)} %feat_hbm.1, f32[9,256,256]{2,1,0:T(8,128)} %bitcast.9, f32[4,256,1024]{2,1,0:T(8,128)} %bitcast.8, f32[9,64,1024]{2,1,0:T(8,128)} %bitcast.10, f32[9,64,1024]{2,1,0:T(8,128)} %bitcast.11), custom_call_target="tpu_custom_call" | custom-call | flops 603979776 | bytes 12582912 | tf_op jit(solution)/shard_map/pallas_call | solution.py:560
  40.2 1.6 %copy.7 = f32[2,16,8,64]{3,2,1,0:T(8,128)} copy(f32[2,16,8,64]{3,2,1,0:T(8,128)} %shard_map.55) | data formatting | bytes 131072

commit v5 on v4

--- a/solution.py
+++ b/solution.py
@@ -491,9 +491,11 @@
         mine[f] = shifted(1 - core, f)
         last(f).start()
 
-    for f in range(fields):
+    collect(0)
+    forward(0, 0)
+    for f in range(1, fields):
         collect(f)
-    for step in range(blocks):
+    for step in range(1, blocks):
         forward(0, step)
     for f in range(fields):
         for step in range(blocks):

time: 41.9 us -> 41.9 us (level)
  no operation moved by 1% of the time
where the time goes in v5:
time: 41.9 us; the launch traced here: 41.8 us
  Pallas kernels  40.2 us (96%)
  local copies, waits for them, and re-layouts  1.57 us (4%)
    pallas_call x1, Pallas kernels, fused_body(): pl.pallas_call(functools.partial(fused, wide), out_shape=jax.ShapeDtypeSt...  40.2 us
    unnamed x1, local copies, waits for them, and re-layouts  1.57 us

profile of v5, /device:TPU:1, one launch (start us, length us, event | category | flops | bytes accessed | tf_op | source)
XLA Modules:
  0.0 41.8 jit_solution(5583266479840540791)
XLA Ops:
  0.0 40.2 %shard_map.55 = f32[2,16,8,64]{3,2,1,0:T(8,128)} custom-call(f32[2,2,16,256]{3,2,1,0:T(8,128)} %feat_hbm.1, f32[9,256,256]{2,1,0:T(8,128)} %bitcast.9, f32[4,256,1024]{2,1,0:T(8,128)} %bitcast.8, f32[9,64,1024]{2,1,0:T(8,128)} %bitcast.10, f32[9,64,1024]{2,1,0:T(8,128)} %bitcast.11), custom_call_target="tpu_custom_call" | custom-call | flops 603979776 | bytes 12582912 | tf_op jit(solution)/shard_map/pallas_call | solution.py:562
  40.2 1.6 %copy.7 = f32[2,16,8,64]{3,2,1,0:T(8,128)} copy(f32[2,16,8,64]{3,2,1,0:T(8,128)} %shard_map.55) | data formatting | bytes 131072
